TPU v7x, 256 devices: a whole 4x4x8 slice. The times are simulated.
256 devices in a mesh: inst: 64 (over y, z, core), tp: 4 (over x).
Axes of the slice: x: 4, y: 4, z: 8, core: 2. Of those that a mesh axis runs over, the one named last changes fastest.
Arguments:
- queries: bfloat16 [8192, 8192], P('inst', 'tp'), may hold values from -130 to 130
- new_keys: bfloat16 [8192, 1024], P('inst', 'tp'), may hold values from -6 to 6
- fresh_values: bfloat16 [8192, 1024], P('inst', 'tp'), may hold values from -6 to 6
- lent_page_pool: bfloat16 [1024, 2, 128, 1024], P('inst', None, None, 'tp'), may hold values from -6 to 6
- page_lender: int32 [2048, 1], P(('inst', 'tp')), may hold values from 0 to 63; in each aligned block of 32 rows (0 to 31, 32 to 63, ...) at most 2 rows name the same one
- page_slot: int32 [2048], P(('inst', 'tp')), may hold values from 0 to 15
- starts: int32 [64], P('inst'), may hold values from 1024 to 4096, as said below
Outputs:
- attended: bfloat16 [8192, 8192], P('inst', 'tp')
Inputs may be any that keep to these rules, and one draw needn't show every extreme that they name: `page_lender`: among the 32 entries of one request at most 2 name the same lender, and some lender holds exactly 2 pages of some request. Some request starts exactly at 4096.
All inputs are finite; a program needn't handle non-finite values.
Results may differ from a plain program's by a relative error of at most 0.0035.
Values may be sent and summed in bfloat16 or wider, within the bound.
A program may use at most 128 MiB of HBM per device.

v0:
```python
import math

import jax
import jax.numpy as jnp
from jax import lax
from jax.sharding import PartitionSpec as P

QUERY_HEADS = 64
KEY_VALUE_HEADS = 8
HEAD_SIZE = 128
CTX_PAGES = 32


def bucket_rank(lenders):
    positions = jnp.arange(lenders.shape[0])
    earlier = (lenders[None, :] == lenders[:, None]) & (positions[None, :] < positions[:, None])
    return jnp.sum(earlier.astype(jnp.int32), axis=1)


def allowed_mask(span_len, page_token_rows, start_pos):
    context_ok = jnp.broadcast_to(
        (jnp.arange(page_token_rows) < start_pos)[None, :], (span_len, page_token_rows)
    )
    causal_ok = jnp.arange(span_len)[None, :] <= jnp.arange(span_len)[:, None]
    return jnp.concatenate([context_ok, causal_ok], axis=1)


def head_weights(queries, joined_keys, allowed, head, query_group_width, head_dim):
    block_queries = lax.dynamic_slice_in_dim(queries, head * head_dim, head_dim, 1)
    block_keys = lax.dynamic_slice_in_dim(
        joined_keys, head // query_group_width * head_dim, head_dim, 1
    )
    scores = jnp.dot(block_queries, block_keys.T, preferred_element_type=jnp.float32) / math.sqrt(
        head_dim
    )
    scores = jnp.where(allowed, scores, -jnp.inf)
    row_peak = jnp.max(scores, axis=1, keepdims=True)
    exponent = jnp.exp(scores - row_peak)
    row_total = jnp.sum(exponent, axis=1, keepdims=True)
    return (exponent.astype(jnp.bfloat16), row_total)


def head_output(weights, row_total, joined_values, head, query_group_width, head_dim):
    block_values = lax.dynamic_slice_in_dim(
        joined_values, head // query_group_width * head_dim, head_dim, 1
    )
    combined = jnp.dot(weights, block_values, preferred_element_type=jnp.float32)
    return (combined / row_total).astype(jnp.bfloat16)


def local(queries, new_keys, fresh_values, lent_page_pool, page_lender, page_slot, starts):
    inst_count = lax.axis_size("inst")
    capacity = max(2, (2 * CTX_PAGES + inst_count - 1) // inst_count)
    query_group_width = QUERY_HEADS // KEY_VALUE_HEADS
    head_dim = HEAD_SIZE
    span_len = queries.shape[0]
    key_width = new_keys.shape[1]
    query_heads = queries.shape[1] // head_dim
    page_token_rows = CTX_PAGES * lent_page_pool.shape[2]
    gathered = (
        lax.all_gather(page_lender[:, 0], "tp", axis=0, tiled=True),
        lax.all_gather(page_slot, "tp", axis=0, tiled=True),
    )
    lenders = gathered[0]
    slots_here = gathered[1]
    bucket_ranks = bucket_rank(lenders)
    targets = lenders * capacity + bucket_ranks
    chosen = targets[:, None] == jnp.arange(inst_count * capacity)[None, :]
    wanted = jnp.sum(jnp.where(chosen, slots_here[:, None], 0), axis=0)
    asked_slots = lax.all_to_all(wanted, "inst", split_axis=0, concat_axis=0, tiled=True)
    served = jnp.take(lent_page_pool, asked_slots, axis=0)
    allowed = allowed_mask(span_len, page_token_rows, starts[0])
    fetched = lax.all_to_all(served, "inst", split_axis=0, concat_axis=0, tiled=True)
    prior_pages = jnp.take(fetched, targets, axis=0)
    joined_keys = jnp.concatenate(
        [prior_pages[:, 0].reshape(page_token_rows, key_width), new_keys], axis=0
    )
    joined_values = jnp.concatenate(
        [prior_pages[:, 1].reshape(page_token_rows, key_width), fresh_values], axis=0
    )

    def one_head(head):
        weights, row_total = head_weights(
            queries, joined_keys, allowed, head, query_group_width, head_dim
        )
        return head_output(weights, row_total, joined_values, head, query_group_width, head_dim)

    attention_output = lax.map(one_head, jnp.arange(query_heads))
    return attention_output.transpose(1, 0, 2).reshape(span_len, query_heads * head_dim)


def solution(mesh):
    in_specs = (
        P("inst", "tp"),
        P("inst", "tp"),
        P("inst", "tp"),
        P("inst", None, None, "tp"),
        P(("inst", "tp"), None),
        P(("inst", "tp")),
        P("inst"),
    )
    out_specs = P("inst", "tp")
    return jax.shard_map(local, mesh=mesh, in_specs=in_specs, out_specs=out_specs, check_vma=False)
```

profile of v0, /device:TPU:1, one launch (start us, length us, event | category | flops | bytes accessed | tf_op | source)
XLA Modules:
  0.0 554.8 jit_solution(2430725257700284930)
XLA Ops:
  0.0 1.4 dynamic-slice
  2.1 0.8 bitcast_dynamic-update-slice_fusion
  2.8 0.8 dynamic-update-slice.1
  3.7 7.7 %all-reduce.2 = (s32[32]{0:T(128)S(1)}, s32[32]{0:T(128)S(1)}) all-reduce(s32[32]{0:T(128)S(1)} %dynamic-update-slice.1, s32[32]{0:T(128)S(1)} %bitcast_dynamic-update-slice_fusion), channel_id=1, replica_groups=mesh['inst'=64,'tp'=4] {'tp'}, use_global_device_ids=true, to_apply=%add.1 | all-reduce | flops 64 | bytes 512
  11.8 23.4 %all_to_all.20 = s32[64,2,1]{1,2,0:T(1,128)S(1)} all-to-all(s32[64,2,1]{1,2,0:T(1,128)S(1)} %bitcast.30), channel_id=1, replica_groups=mesh['inst'=64,'tp'=4] {'inst'}, dimensions={0} | all-to-all | bytes 1024 | tf_op jit(solution)/shard_map/all_to_all | solution.py:70
  35.4 0.6 broadcast.67
  36.0 0.8 reduce.5
  36.9 7.8 %gather_fusion = bf16[128,2,128,256]{3,2,1,0:T(8,128)(2,1)} fusion(bf16[16,2,128,256]{3,2,1,0:T(8,128)(2,1)S(1)} %copy-done, s32[1024]{0:T(1024)S(1)} %pad_clamp_fusion.1), kind=kCustom, calls=%fused_computation | custom fusion | bytes 33554944 | tf_op jit(solution)/shard_map/jit(_take)/gather | solution.py:71
  44.8 14.2 %broadcast_select_fusion = bf16[128,2,128,256]{3,2,1,0:T(8,128)(2,1)} fusion(bf16[128,2,128,256]{3,2,1,0:T(8,128)(2,1)} %gather_fusion, pred[128]{0:T(512)(128)(4,1)S(1)} %compare_and_fusion), kind=kLoop, calls=%fused_computation.17 | loop fusion | flops 8388608 | bytes 33554560 | tf_op jit(solution)/shard_map/jit(_take)/select_n | solution.py:71
  58.9 5.9 %all-to-all-start.1 = ((bf16[128,2,128,256]{3,2,1,0:T(8,128)(2,1)}), bf16[128,2,128,256]{3,2,1,0:T(8,128)(2,1)}, u32[]{:S(2)}, u32[]{:S(2)}) async-start(bf16[128,2,128,256]{3,2,1,0:T(8,128)(2,1)} %broadcast_select_fusion), calls=%async_computation.1 | async-start | bytes 33554432 | tf_op jit(solution)/shard_map/all_to_all | solution.py:73
  65.7 364.7 %all-to-all-done.1 = bf16[128,2,128,256]{3,2,1,0:T(8,128)(2,1)} async-done(((bf16[128,2,128,256]{3,2,1,0:T(8,128)(2,1)}), bf16[128,2,128,256]{3,2,1,0:T(8,128)(2,1)}, u32[]{:S(2)}, u32[]{:S(2)}) %all-to-all-start.1) | async-done | bytes 16777248 | tf_op jit(solution)/shard_map/all_to_all | solution.py:73
  430.4 8.5 %gather_fusion.1 = bf16[32,2,128,256]{3,2,1,0:T(8,128)(2,1)} fusion(bf16[128,2,128,256]{3,2,1,0:T(8,128)(2,1)} %all-to-all-done.1, s32[1024]{0:T(1024)S(1)} %pad_clamp_fusion), kind=kCustom, calls=%fused_computation.1 | custom fusion | bytes 8388736 | tf_op jit(solution)/shard_map/jit(_take)/gather | solution.py:74
  438.9 2.6 broadcast_select_fusion.1
  442.4 2.3 pad_maximum_fusion
  444.7 108.3 %while.12 = (s32[]{:T(128)}, bf16[16,128,128]{2,1,0:T(8,128)(2,1)S(1)}, s32[16]{0:T(128)S(1)}, bf16[128,2048]{1,0:T(8,128)(2,1)}, bf16[4224,256]{1,0:T(8,128)(2,...) while((s32[]{:T(128)}, ...), condition=%wide.region_5.6_spmd, body=%wide.region_2.0_spmd.sunk | while | flops 280641312 | bytes 17910712 | solution.py:88
  444.7 0.6 dynamic_slice.42
  448.4 2.0 fusion.25
  450.9 0.6 fusion.27
  451.5 0.6 dynamic_slice.42
  455.2 2.0 fusion.25
  457.7 0.6 fusion.27
  458.3 0.6 dynamic_slice.42
  462.0 2.0 fusion.25
  464.5 0.6 fusion.27
  465.0 0.6 dynamic_slice.42
  468.7 2.0 fusion.25
  471.2 0.6 fusion.27
  471.8 0.6 dynamic_slice.42
  475.5 2.0 fusion.25
  478.0 0.6 fusion.27
  478.6 0.6 dynamic_slice.42
  482.3 2.0 fusion.25
  484.8 0.6 fusion.27
  485.4 0.6 dynamic_slice.42
  489.0 2.0 fusion.25
  491.5 0.6 fusion.27
  492.1 0.6 dynamic_slice.42
  495.8 2.0 fusion.25
  498.3 0.6 fusion.27
  498.9 0.6 dynamic_slice.42
  502.6 2.0 fusion.25
  505.1 0.6 fusion.27
  505.7 0.6 dynamic_slice.42
  509.4 2.0 fusion.25
  511.8 0.6 fusion.27
  512.4 0.6 dynamic_slice.42
  516.1 2.0 fusion.25
  518.6 0.6 fusion.27
  519.2 0.6 dynamic_slice.42
  522.9 2.0 fusion.25
  525.4 0.6 fusion.27
  526.0 0.6 dynamic_slice.42
  529.7 2.0 fusion.25
  532.2 0.6 fusion.27
  532.7 0.6 dynamic_slice.42
  536.4 2.0 fusion.25
  538.9 0.6 fusion.27
  539.5 0.6 dynamic_slice.42
  543.2 2.0 fusion.25
  545.7 0.6 fusion.27
  546.3 0.6 dynamic_slice.42
  550.0 2.0 fusion.25
  553.1 0.9 copy_bitcast_fusion
  553.9 0.9 copy-done.1
  (76 shorter events, 9.7 us)
Async XLA Ops:
  0.0 36.9 %copy-start = (bf16[16,2,128,256]{3,2,1,0:T(8,128)(2,1)S(1)}, bf16[16,2,128,256]{3,2,1,0:T(8,128)(2,1)}, u32[]{:S(2)}) copy-start(bf16[16,2,128,256]{3,2,1,0:T(8,128)(2,1)} %param.12) | copy-start | bytes 6291460
  58.9 371.5 %all-to-all-start.1 = ((bf16[128,2,128,256]{3,2,1,0:T(8,128)(2,1)}), bf16[128,2,128,256]{3,2,1,0:T(8,128)(2,1)}, u32[]{:S(2)}, u32[]{:S(2)}) async-start(bf16[128,2,128,256]{3,2,1,0:T(8,128)(2,1)} %broadcast_select_fusion), calls=%async_computation.1 | async-start | bytes 33554432 | tf_op jit(solution)/shard_map/all_to_all | solution.py:73
  441.6 0.8 copy-start.3
  441.6 0.9 copy-start.4
  448.4 2.5 copy-start.2
  455.2 2.5 copy-start.2
  462.0 2.5 copy-start.2
  468.7 2.5 copy-start.2
  475.5 2.5 copy-start.2
  482.3 2.5 copy-start.2
  489.0 2.5 copy-start.2
  495.8 2.5 copy-start.2
  502.6 2.5 copy-start.2
  509.3 2.5 copy-start.2
  516.1 2.5 copy-start.2
  522.9 2.5 copy-start.2
  529.7 2.5 copy-start.2
  536.4 2.5 copy-start.2
  543.2 2.5 copy-start.2
  550.0 2.5 copy-start.2
  553.1 1.8 copy-start.1
where the time goes:
time: 556 us; the launch traced here: 555 us
  waiting for transfers between devices  365 us (66%)
  loops' own time  49.7 us (9%)
  matrix products  41.4 us (7%)
  local copies, waits for them, and re-layouts  33 us (6%)
  blocking collectives  31.1 us (6%)
  other arithmetic  27.7 us (5%)
  starting transfers between devices  5.88 us (1%)
    all_to_all x1, waiting for transfers between devices, local(): lax.all_to_all(served, 'inst', split_axis=0, concat_axis=0, tiled=True)  365 us
    another operation x1, loops' own time, local(): attention_output = lax.map(one_head, jnp.arange(query_heads))  49.7 us
    dot_general x16, matrix products, head_weights(): jnp.dot(block_queries, block_keys.T, preferred_element_type=jnp.float32)  32.3 us
    all_to_all x1, blocking collectives, local(): lax.all_to_all(wanted, 'inst', split_axis=0, concat_axis=0, tiled=True)  23.4 us
    select_n x2, other arithmetic, local(): served = jnp.take(lent_page_pool, asked_slots, axis=0)  14.2 us
  transfers between devices with their start and end apart: 1, of which 1 were waited for; matrix products, arithmetic and copies ran while one was open for 0% of the time, Pallas kernels for 0%

commit v1 on v0

v1 whole, which is shorter than its diff:
```python
import functools
import math

import jax
import jax.numpy as jnp
from jax import lax
from jax.experimental import pallas as pl
from jax.experimental.pallas import tpu as pltpu
from jax.sharding import PartitionSpec as P

MESH = pl.DeviceIdType.MESH
HEAD = 128
PAGE = 128
NY, NZ, NX = 4, 8, 4
CHIPS = NY * NZ
SLOTS = 16
CTX_PAGES = 32
ROWS = PAGE // NZ
GROUP = 8
KV_HEADS = 2
SCALE = math.log2(math.e) / math.sqrt(HEAD)


def dz_of(i):
    return (i % 2) * ((i + 1) // 2) + (1 - i % 2) * ((NZ - i // 2) % NZ)


def scores(q, k):
    return lax.dot_general(q, k, (((1,), (1,)), ((), ())), preferred_element_type=jnp.float32) * SCALE


def kernel(
    start_ref, q_ref, nk_ref, nv_ref, pool_ref, tab_ref, out_ref,
    stage1, frag, stage2, recv2, tabx, tabj, tabsum, tabs, m_ref, l_ref, acc_ref,
    load_sem, own_sem, smem_sem, xs, xr, ts, tr, s1, r1, fs, fr, s2, r2,
):
    inst, x = lax.axis_index("inst"), lax.axis_index("tp")
    core, chip = inst % 2, inst // 2
    z, y = chip % NZ, chip // NZ
    sibling = (chip * 2 + 1 - core, x)

    def chip_at(i, dy, sign):
        dz = dz_of(i)
        return ((y + sign * dy + NY) % NY) * NZ + (z + sign * dz + NZ) % NZ

    def remote(src, dst, ss, rs, device):
        return pltpu.make_async_remote_copy(
            src_ref=src, dst_ref=dst, send_sem=ss, recv_sem=rs, device_id=device, device_id_type=MESH
        )

    def each(first, body):
        for dy in range(0 if first else 1, NY):
            body(0, dy)

        @pl.loop(1, NZ)
        def _(i):
            for dy in range(NY):
                body(i, dy)

    def load(t):
        yy, zz = t // NZ, t % NZ
        return pltpu.make_async_copy(
            pool_ref.at[:, yy % 2, pl.ds(zz * ROWS, ROWS), pl.ds((yy // 2) * HEAD, HEAD)], stage1.at[t], load_sem
        )

    for t in range(CHIPS):
        load(t).start()

    barrier = pltpu.get_barrier_semaphore()

    def greet(i, dy):
        pl.semaphore_signal(barrier, inc=1, device_id=(chip_at(i, dy, 1) * 2 + core, x), device_id_type=MESH)

    each(False, greet)
    pl.semaphore_signal(barrier, inc=1, device_id=sibling, device_id_type=MESH)
    for d in range(1, NX):
        pl.semaphore_signal(barrier, inc=1, device_id=(inst, (x + d) % NX), device_id_type=MESH)
    pl.semaphore_wait(barrier, CHIPS - 1 + 1 + NX - 1)

    lane = lax.broadcasted_iota(jnp.int32, (8, 128), 1)
    tabx[0] = jnp.where(lane == chip * NX + x, tab_ref[...], 0)

    def table_x(d):
        return remote(tabx.at[0], tabx.at[d], xs.at[d], xr.at[d], (inst, (x + d) % NX))

    for d in range(1, NX):
        table_x(d).start()

    pltpu.make_async_copy(stage1, stage1, load_sem).wait()

    def spread(i, dy):
        t = chip_at(i, dy, 1)
        return remote(
            stage1.at[t], frag.at[pl.ds(inst * SLOTS, SLOTS)], s1.at[i * NY + dy], r1.at[i * NY + dy], (t * 2 + core, x)
        )

    each(False, lambda i, dy: spread(i, dy).start())
    own = pltpu.make_async_copy(stage1.at[chip], frag.at[pl.ds(inst * SLOTS, SLOTS)], own_sem)
    own.start()

    for d in range(1, NX):
        table_x(d).wait()
    tabj[0] = tabx[0] + tabx[1] + tabx[2] + tabx[3]

    def table_j(i, dy):
        s = i * NY + dy
        return remote(tabj.at[0], tabj.at[s], ts.at[s], tr.at[s], (chip_at(i, dy, 1) * 2 + core, x))

    each(False, lambda i, dy: table_j(i, dy).start())

    row = lax.broadcasted_iota(jnp.int32, (PAGE, PAGE), 0)
    col = lax.broadcasted_iota(jnp.int32, (PAGE, PAGE), 1)
    for h in range(KV_HEADS):
        heads = pl.ds(h * HEAD, HEAD)

        @pl.loop(0, GROUP)
        def _(g):
            n = h * GROUP + g
            q = q_ref[:, pl.ds(pl.multiple_of(n * HEAD, HEAD), HEAD)]
            s = jnp.where(col <= row, scores(q, nk_ref[:, heads]), -jnp.inf)
            m = jnp.broadcast_to(jnp.max(s, axis=1, keepdims=True), s.shape)
            p = jnp.exp2(s - m)
            m_ref[n] = m
            l_ref[n] = p
            acc_ref[n] = jnp.dot(p.astype(jnp.bfloat16), nv_ref[:, heads], preferred_element_type=jnp.float32)

    own.wait()

    def forward(i, dy):
        lender = chip_at(i, dy, -1) * 2 + core
        part = frag.at[pl.ds(lender * SLOTS, SLOTS)]
        return remote(part, part, fs.at[i * NY + dy], fr.at[i * NY + dy], sibling)

    def pass_on(i, dy):
        if not (isinstance(i, int) and i == 0 and dy == 0):
            spread(i, dy).wait_recv()
        forward(i, dy).start()

    each(True, pass_on)

    each(False, lambda i, dy: table_j(i, dy).wait())
    total = tabj[0]
    for s in range(1, CHIPS):
        total = total + tabj[s]
    tabsum[...] = total
    to_smem = pltpu.make_async_copy(tabsum, tabs, smem_sem)
    to_smem.start()
    to_smem.wait()

    each(True, lambda i, dy: forward(i, dy).wait())

    def deliver(i, dy):
        s = i * NY + dy
        return remote(stage2.at[s], recv2.at[s], s2.at[s], r2.at[s], (chip_at(i, dy, 1) * 2 + core, x))

    def pick(i, dy):
        s = i * NY + dy
        there = chip_at(i, dy, 1)
        mine = isinstance(i, int) and i == 0 and dy == 0
        for p in range(CTX_PAGES):
            tile = frag[tabs[p % 8, there * NX + p // 8]]
            if mine:
                recv2[0, p] = tile
            else:
                stage2[s, p] = tile
        if not mine:
            deliver(i, dy).start()

    each(False, pick)
    pick(0, 0)

    start = start_ref[0]
    keys = CTX_PAGES * ROWS
    at = lax.broadcasted_iota(jnp.int32, (1, keys), 1)

    def attend(i):
        base = ((z - dz_of(i) + NZ) % NZ) * ROWS
        allowed = at // ROWS * PAGE + at % ROWS + base < start
        for h in range(KV_HEADS):
            k_slot = i * NY + (y - 2 * h + NY) % NY
            v_slot = i * NY + (y - 2 * h - 1 + NY) % NY
            k = recv2[k_slot].reshape(keys, HEAD)
            v = recv2[v_slot].reshape(keys, HEAD)

            @pl.loop(0, GROUP)
            def _(g):
                n = h * GROUP + g
                q = q_ref[:, pl.ds(pl.multiple_of(n * HEAD, HEAD), HEAD)]
                s = jnp.where(allowed, scores(q, k), -jnp.inf)
                parts = [s[:, j * HEAD:(j + 1) * HEAD] for j in range(keys // HEAD)]
                m_old = m_ref[n]
                m = jnp.maximum(m_old, jnp.max(functools.reduce(jnp.maximum, parts), axis=1, keepdims=True))
                alpha = jnp.exp2(m_old - m)
                ps = [jnp.exp2(part - m) for part in parts]
                m_ref[n] = m
                l_ref[n] = l_ref[n] * alpha + functools.reduce(jnp.add, ps)
                p = jnp.concatenate([part.astype(jnp.bfloat16) for part in ps], axis=1)
                acc_ref[n] = acc_ref[n] * alpha + jnp.dot(p, v, preferred_element_type=jnp.float32)

    for dy in range(1, NY):
        deliver(0, dy).wait_recv()
    attend(0)

    @pl.loop(1, NZ)
    def _(i):
        for dy in range(NY):
            deliver(i, dy).wait_recv()
        attend(i)

    for n in range(KV_HEADS * GROUP):
        total = jnp.sum(l_ref[n], axis=1, keepdims=True)
        out_ref[:, n * HEAD:(n + 1) * HEAD] = (acc_ref[n] / total).astype(jnp.bfloat16)

    each(False, lambda i, dy: spread(i, dy).wait_send())
    each(False, lambda i, dy: deliver(i, dy).wait_send())


def local(queries, new_keys, fresh_values, lent_page_pool, page_lender, page_slot, starts):
    pages = page_lender * SLOTS + page_slot[:, None]
    table = jnp.broadcast_to(pages, (8, 128))
    vmem = pl.BlockSpec(memory_space=pltpu.VMEM)
    dma = pltpu.SemaphoreType.DMA
    heads = KV_HEADS * GROUP
    bf16, f32, i32 = jnp.bfloat16, jnp.float32, jnp.int32
    return pl.pallas_call(
        kernel,
        out_shape=jax.ShapeDtypeStruct(queries.shape, bf16),
        in_specs=[
            pl.BlockSpec(memory_space=pltpu.SMEM), vmem, vmem, vmem, pl.BlockSpec(memory_space=pl.ANY), vmem,
        ],
        out_specs=vmem,
        scratch_shapes=[
            pltpu.VMEM((CHIPS, SLOTS, ROWS, HEAD), bf16),
            pltpu.VMEM((CHIPS * 2 * SLOTS, ROWS, HEAD), bf16),
            pltpu.VMEM((CHIPS, CTX_PAGES, ROWS, HEAD), bf16),
            pltpu.VMEM((CHIPS, CTX_PAGES, ROWS, HEAD), bf16),
            pltpu.VMEM((NX, 8, 128), i32),
            pltpu.VMEM((CHIPS, 8, 128), i32),
            pltpu.VMEM((8, 128), i32),
            pltpu.SMEM((8, 128), i32),
            pltpu.VMEM((heads, PAGE, HEAD), f32),
            pltpu.VMEM((heads, PAGE, HEAD), f32),
            pltpu.VMEM((heads, PAGE, HEAD), f32),
            dma, dma, dma,
            dma((NX,)), dma((NX,)),
            dma((CHIPS,)), dma((CHIPS,)),
            dma((CHIPS,)), dma((CHIPS,)),
            dma((CHIPS,)), dma((CHIPS,)),
            dma((CHIPS,)), dma((CHIPS,)),
        ],
        compiler_params=pltpu.CompilerParams(
            collective_id=0, has_side_effects=True, vmem_limit_bytes=48 * 1024 * 1024
        ),
        cost_estimate=pl.CostEstimate(
            flops=4 * heads * PAGE * HEAD * (CTX_PAGES + 1) * PAGE,
            bytes_accessed=4 << 20,
            transcendentals=heads * PAGE * (CTX_PAGES + 1) * PAGE,
        ),
    )(starts, queries, new_keys, fresh_values, lent_page_pool, table)


def solution(mesh):
    in_specs = (
        P("inst", "tp"),
        P("inst", "tp"),
        P("inst", "tp"),
        P("inst", None, None, "tp"),
        P(("inst", "tp"), None),
        P(("inst", "tp")),
        P("inst"),
    )
    return jax.shard_map(local, mesh=mesh, in_specs=in_specs, out_specs=P("inst", "tp"), check_vma=False)
```

time: 556 us -> 178 us (0.32)
  the two profiles are of different devices: /device:TPU:1 before, /device:TPU:50 now
where the time goes in v1:
time: 178 us; the launch traced here: 177 us
  Pallas kernels  171 us (96%)
  local copies, waits for them, and re-layouts  5.18 us (3%)
    pallas_call x1, Pallas kernels, local(): pl.pallas_call(kernel, out_shape=jax.ShapeDtypeStruct(queries.shape, bf16...  171 us
    unnamed x9, local copies, waits for them, and re-layouts  5.11 us

profile of v1, /device:TPU:50, one launch (start us, length us, event | category | flops | bytes accessed | tf_op | source)
XLA Modules:
  0.0 177.3 jit_solution(17823647591411469436)
XLA Ops:
  0.7 0.7 fusion
  1.3 0.1 broadcast_in_dim.12.tab_ref
  1.4 0.0 copy-start
  1.4 1.6 copy-done
  3.0 0.0 copy-start.1
  3.0 1.0 copy-done.1
  4.0 0.0 copy-start.2
  4.0 0.8 copy-done.2
  4.9 0.0 copy-start.3
  4.9 0.8 copy-done.3
  5.7 170.8 %shard_map.73 = bf16[128,2048]{1,0:T(8,128)(2,1)S(1)} custom-call(s32[1]{0:T(128)S(6)} %copy.9.start_ref, bf16[128,2048]{1,0:T(8,128)(2,1)S(1)} %copy-done.1, bf16[128,256]{1,0:T(8,128)(2,1)S(1)} %copy-done.2, bf16[128,256]{1,0:T(8,128)(2,1)S(1)} %copy-done.3, bf16[16,2,128,256]{3,2,1,0:T(8,128)(2,1)S(1)} %copy-done, s32[8,128]{1,0:T(8,128)S(1)} %broadcast_in_dim.12.tab_ref), custom_call_target="tpu_custom_call" | custom-call | flops 4429185024 | bytes 4194304 | tf_op jit(solution)/shard_map/pallas_call | solution.py:225
  176.5 0.8 copy.10
Async XLA Ops:
  1.4 1.6 copy-start
  3.0 1.0 copy-start.1
  4.0 0.8 copy-start.2
  4.9 0.8 copy-start.3

commit v2 on v1

--- a/solution.py
+++ b/solution.py
@@ -18,6 +18,8 @@
 ROWS = PAGE // NZ
 GROUP = 8
 KV_HEADS = 2
+UNROLL = 1
+PAIR = 8
 SCALE = math.log2(math.e) / math.sqrt(HEAD)
 
 
@@ -29,7 +31,7 @@
     return lax.dot_general(q, k, (((1,), (1,)), ((), ())), preferred_element_type=jnp.float32) * SCALE
 
 
-def kernel(
+def wide_kernel(
     start_ref, q_ref, nk_ref, nv_ref, pool_ref, tab_ref, out_ref,
     stage1, frag, stage2, recv2, tabx, tabj, tabsum, tabs, m_ref, l_ref, acc_ref,
     load_sem, own_sem, smem_sem, xs, xr, ts, tr, s1, r1, fs, fr, s2, r2,
@@ -215,7 +217,442 @@
     each(False, lambda i, dy: deliver(i, dy).wait_send())
 
 
-def local(queries, new_keys, fresh_values, lent_page_pool, page_lender, page_slot, starts):
+ROUNDS = 4
+OPEN = 2
+PLANE = 2 * NY * SLOTS
+WIDTH = (84, 72, 56, 24)
+OFF = (0, 128, 200, 256)
+TOTAL = OFF[-1] + WIDTH[-1]
+JOINED = PLANE + 2 * TOTAL
+HOPS = len(WIDTH)
+STEP = (1, -1)
+
+
+def width(r, t):
+    return PLANE if t == 1 and r < OPEN else WIDTH[t - 1]
+
+
+def base_of(s, t):
+    return PLANE + s * TOTAL + OFF[t - 1]
+
+
+def narrow_kernel(
+    start_ref, tab_ref, q_any, nk_any, nv_any, pool_ref, out_ref, over_ref,
+    q_ref, nk_ref, nv_ref, stage, home, arrive, sbuf, join, ybuf, recv,
+    tabx, tabz, tabp, tabv, tabs, need, member, before, place, mat, metav, meta, plist, m_ref, l_ref, acc_ref,
+    in_sem, load_sem, own_sem, smem_sem, xs, xr, zs, zr, ps, pr, hs, hr, rs, rr, ys, yr,
+):
+    inst, x = lax.axis_index("inst"), lax.axis_index("tp")
+    core, chip = inst % 2, inst // 2
+    z, y = chip % NZ, chip // NZ
+    i32 = jnp.int32
+
+    def device(dy, dz, dc):
+        return ((((y + dy) % NY) * NZ + (z + dz + NZ) % NZ) * 2 + (core + dc) % 2, x)
+
+    def remote(src, dst, ss, rs_, dev):
+        return pltpu.make_async_remote_copy(
+            src_ref=src, dst_ref=dst, send_sem=ss, recv_sem=rs_, device_id=dev, device_id_type=MESH
+        )
+
+    inputs = [
+        pltpu.make_async_copy(src, dst, in_sem.at[n])
+        for n, (src, dst) in enumerate(((q_any, q_ref), (nk_any, nk_ref), (nv_any, nv_ref)))
+    ]
+    for yy in range(NY):
+        for tb in range(NZ):
+            pltpu.make_async_copy(
+                pool_ref.at[:, yy % 2, pl.ds(tb * ROWS, ROWS), pl.ds((yy // 2) * HEAD, HEAD)],
+                stage.at[yy, tb % 2, tb // 2], load_sem,
+            ).start()
+    for copy in inputs:
+        copy.start()
+
+    barrier = pltpu.get_barrier_semaphore()
+
+    def greet(dev):
+        pl.semaphore_signal(barrier, inc=1, device_id=dev, device_id_type=MESH)
+
+    for d in range(1, NX):
+        greet((inst, (x + d) % NX))
+
+    @pl.loop(1, NZ)
+    def _(d):
+        greet(device(0, d, 0))
+
+    @pl.loop(1, 2 * NY)
+    def _(k):
+        greet(device(k // 2, 0, k % 2))
+
+    pl.semaphore_wait(barrier, NX - 1 + NZ - 1 + 2 * NY - 1)
+
+    row = lax.broadcasted_iota(i32, (8, 128), 0)
+    lane = lax.broadcasted_iota(i32, (8, 128), 1)
+    wanted = (lane == chip * NX + x) & ((x * 8 + row) * PAGE < start_ref[0])
+    tabx[0] = jnp.where(wanted, tab_ref[...], 0)
+
+    def table_x(d):
+        return remote(tabx.at[0], tabx.at[d], xs.at[d], xr.at[d], (inst, (x + d) % NX))
+
+    for d in range(1, NX):
+        table_x(d).start()
+
+    pltpu.make_async_copy(stage, stage, load_sem).wait()
+    here = pl.ds((y * 2 + core) * SLOTS, SLOTS)
+
+    def spread(r, k):
+        dy, dc = k // 2, k % 2
+        return remote(
+            stage.at[(y + dy) % NY, (core + dc) % 2, r], home[r].at[here], hs.at[r, k], hr.at[r, k], device(dy, 0, dc)
+        )
+
+    def own(r):
+        return pltpu.make_async_copy(stage.at[y, core, r], home[r].at[here], own_sem.at[r])
+
+    def spread_all(r):
+        own(r).start()
+
+        @pl.loop(1, 2 * NY)
+        def _(k):
+            spread(r, k).start()
+
+    def hop(r, s, t):
+        src = home[r] if width(r, t) == PLANE else sbuf.at[r, s, pl.ds(OFF[t - 1], WIDTH[t - 1])]
+        return remote(src, arrive[r][s][t - 1], rs.at[r, s, t - 1], rr.at[r, s, t - 1], device(0, STEP[s], 0))
+
+    def ring(r, t):
+        if t == 1:
+            own(r).wait()
+
+            @pl.loop(1, 2 * NY)
+            def _(k):
+                spread(r, k).wait_recv()
+
+        lists = 3 if r < OPEN else 1
+        for s in range(2):
+            source = home[r]
+            if t > 1:
+                hop(r, s, t - 1).wait_recv()
+                source = arrive[r][s][t - 2]
+            if width(r, t) < PLANE:
+
+                @pl.loop(0, WIDTH[t - 1] // 4)
+                def _(kk):
+                    for u in range(4):
+                        k = kk * 4 + u
+                        sbuf[r, s, OFF[t - 1] + k] = source[meta[lists, s * HOPS + t - 1, k]]
+
+            hop(r, s, t).start()
+
+    spread_all(0)
+
+    for d in range(1, NX):
+        table_x(d).wait()
+    tabz[0] = tabx[0] + tabx[1] + tabx[2] + tabx[3]
+
+    def table_z(d):
+        return remote(tabz.at[0], tabz.at[d], zs.at[d], zr.at[d], device(0, d, 0))
+
+    @pl.loop(1, NZ)
+    def _(d):
+        table_z(d).start()
+
+    @pl.loop(1, NZ)
+    def _(d):
+        table_z(d).wait()
+
+    tabp[0] = functools.reduce(jnp.add, [tabz[d] for d in range(NZ)])
+
+    def table_p(k):
+        return remote(tabp.at[0], tabp.at[k], ps.at[k], pr.at[k], device(k // 2, 0, k % 2))
+
+    @pl.loop(1, 2 * NY)
+    def _(k):
+        table_p(k).start()
+
+    spread_all(1)
+    ring(0, 1)
+
+    @pl.loop(1, 2 * NY)
+    def _(k):
+        table_p(k).wait()
+
+    for dc in range(2):
+        tabv[dc] = functools.reduce(jnp.add, [tabp[2 * dy + dc] for dy in range(NY)])
+    to_smem = pltpu.make_async_copy(tabv, tabs, smem_sem.at[0])
+    to_smem.start()
+    ring(1, 1)
+    for r in range(2, ROUNDS):
+        spread_all(r)
+    to_smem.wait()
+
+    number = row * PLANE + lane + 1
+
+    @pl.loop(0, NZ)
+    def _(d):
+        hit = jnp.zeros((8, 128), i32)
+        for dc in range(2):
+            for yy in range(NY):
+                for xx in range(NX):
+                    for e in range(8):
+                        hit = jnp.where(number == tabs[dc, e, (yy * NZ + d) * NX + xx], 1, hit)
+        need[d] = hit
+
+    def ahead(k):
+        return functools.reduce(jnp.add, [jnp.where(row == (d - k) % NZ, need[d], 0) for d in range(NZ)])
+
+    even = lane % 2 == 0
+    far = ahead(NZ // 2)
+    over = None
+    for s in range(2):
+        users = [jnp.where(even if s == 0 else ~even, far, 0)]
+        for t in range(HOPS - 1, 0, -1):
+            users.insert(0, users[0] | ahead(t if s == 0 else NZ - t))
+        for t in range(1, HOPS + 1):
+            n = s * HOPS + t - 1
+            count = users[t - 1]
+            shift = 1
+            while shift < 128:
+                count = count + jnp.where(lane >= shift, pltpu.roll(count, shift, 1), 0)
+                shift *= 2
+            excess = count - WIDTH[t - 1]
+            over = excess if over is None else jnp.maximum(over, excess)
+            count = count - users[t - 1]
+            member[n] = users[t - 1]
+            before[n] = count
+            place[n] = jnp.minimum(count, WIDTH[t - 1] - 1)
+    over_ref[0, 0] = jnp.max(over)
+
+    for variant in range(2):
+        where_to = jnp.where(row == z, lane, 0)
+        for s in range(2):
+            for t in range(1, HOPS + 1):
+                mine = row == (z - STEP[s] * t + NZ) % NZ
+                if t == HOPS:
+                    mine = mine & (even if s == 0 else ~even)
+                at_hop = lane if variant and t == 1 else place[s * HOPS + t - 1]
+                where_to = where_to + jnp.where(mine, base_of(s, t) + at_hop, 0)
+        metav[2 * variant] = where_to
+
+    mat[...] = jnp.zeros_like(mat)
+    for s in range(2):
+        for t in range(1, HOPS + 1):
+            n = s * HOPS + t - 1
+            o = pl.ds((z - STEP[s] * (t - 1) + NZ) % NZ, 1)
+            mat[n:n + 1] = jnp.where(member[n, o] > 0, before[n, o], 999)
+            mat[8 + n:9 + n] = lane[0:1] if t == 1 else place[n - 1, o]
+    turned = mat[...].T
+    lanes = lax.broadcasted_iota(i32, (128, 128), 1)
+    pages = lax.broadcasted_iota(i32, (128, 128), 0)
+    for n in range(2 * HOPS):
+        goes = turned[:, n:n + 1] == lanes
+        row_n = jnp.sum(jnp.where(goes, turned[:, 8 + n:9 + n], 0), axis=0, keepdims=True)
+        metav[1, n:n + 1] = row_n
+        if n % HOPS == 1:
+            row_n = jnp.sum(jnp.where(goes, pages, 0), axis=0, keepdims=True)
+        metav[3, n:n + 1] = row_n
+    to_smem2 = pltpu.make_async_copy(metav, meta, smem_sem.at[1])
+    to_smem2.start()
+    to_smem2.wait()
+
+    def find():
+        @pl.loop(0, 2 * NY)
+        def _(k):
+            column = (((y + k // 2) % NY) * NZ + z) * NX
+            for p in range(CTX_PAGES):
+                e = jnp.maximum(tabs[k % 2, p % 8, column + p // 8] - 1, 0)
+                for variant in range(2):
+                    plist[variant * 2 * NY + k, p] = meta[2 * variant, e // PLANE, e % PLANE]
+
+    def deliver(r, k):
+        return remote(ybuf.at[r, k], recv.at[r, k], ys.at[r, k], yr.at[r, k], device(k // 2, 0, k % 2))
+
+    def hand_out(r):
+        for s in range(2):
+            hop(r, s, HOPS).wait_recv()
+
+        @pl.loop(0, PLANE // 8)
+        def _(j):
+            join[pl.ds(j * 8, 8)] = home[r][pl.ds(j * 8, 8)]
+
+        for s in range(2):
+            for t in range(1, HOPS + 1):
+
+                @pl.loop(0, width(r, t) // 4)
+                def _(j):
+                    join[pl.ds(base_of(s, t) + j * 4, 4)] = arrive[r][s][t - 1][pl.ds(j * 4, 4)]
+
+        lists = 2 * NY if r < OPEN else 0
+
+        def pick(k):
+            for p in range(CTX_PAGES):
+                ybuf[r, k, p] = join[plist[lists + k, p]]
+            deliver(r, k).start()
+
+        @pl.loop(1, NY)
+        def _(dy):
+            pick(2 * dy)
+
+        @pl.loop(0, NY)
+        def _(dy):
+            pick(2 * dy + 1)
+
+        for p in range(CTX_PAGES):
+            recv[r, 0, p] = join[plist[lists, p]]
+
+    def new_tokens():
+        for copy in inputs:
+            copy.wait()
+        rows_ = lax.broadcasted_iota(i32, (PAGE, PAGE), 0)
+        cols_ = lax.broadcasted_iota(i32, (PAGE, PAGE), 1)
+        for h in range(KV_HEADS):
+            heads = pl.ds(h * HEAD, HEAD)
+
+            @pl.loop(0, GROUP, unroll=UNROLL)
+            def _(g):
+                n = h * GROUP + g
+                q = q_ref[:, pl.ds(pl.multiple_of(n * HEAD, HEAD), HEAD)]
+                s = jnp.where(cols_ <= rows_, scores(q, nk_ref[:, heads]), -jnp.inf)
+                m = jnp.broadcast_to(jnp.max(s, axis=1, keepdims=True), s.shape)
+                p = jnp.exp2(s - m)
+                m_ref[n] = m
+                l_ref[n] = p
+                acc_ref[n] = jnp.dot(p.astype(jnp.bfloat16), nv_ref[:, heads], preferred_element_type=jnp.float32)
+
+    start = start_ref[0]
+    keys = CTX_PAGES * ROWS
+    at = lax.broadcasted_iota(i32, (1, keys), 1)
+
+    def attend(r, dc, h):
+        tb = 2 * r + (core + dc) % 2
+        allowed = at // ROWS * PAGE + at % ROWS + tb * ROWS < start
+        k = recv[r, (y - 2 * h + NY) % NY * 2 + dc].reshape(keys, HEAD)
+        v = recv[r, (y - 2 * h - 1 + NY) % NY * 2 + dc].reshape(keys, HEAD)
+
+        @pl.loop(0, GROUP // PAIR, unroll=UNROLL)
+        def _(g):
+            n = h * GROUP + g * PAIR
+            wide_row = (PAIR * PAGE, HEAD)
+            q = jnp.concatenate(
+                [q_ref[:, pl.ds(pl.multiple_of((n + e) * HEAD, HEAD), HEAD)] for e in range(PAIR)], axis=0
+            )
+            s = jnp.where(allowed, scores(q, k), -jnp.inf)
+            parts = [s[:, j * HEAD:(j + 1) * HEAD] for j in range(keys // HEAD)]
+            m_old = m_ref[pl.ds(n, PAIR)].reshape(wide_row)
+            m = jnp.maximum(m_old, jnp.max(functools.reduce(jnp.maximum, parts), axis=1, keepdims=True))
+            alpha = jnp.exp2(m_old - m)
+            ps_ = [jnp.exp2(part - m) for part in parts]
+            m_ref[pl.ds(n, PAIR)] = m.reshape(PAIR, PAGE, HEAD)
+            l = l_ref[pl.ds(n, PAIR)].reshape(wide_row) * alpha + functools.reduce(jnp.add, ps_)
+            l_ref[pl.ds(n, PAIR)] = l.reshape(PAIR, PAGE, HEAD)
+            p = jnp.concatenate([part.astype(jnp.bfloat16) for part in ps_], axis=1)
+            acc = acc_ref[pl.ds(n, PAIR)].reshape(wide_row) * alpha
+            acc = acc + jnp.dot(p, v, preferred_element_type=jnp.float32)
+            acc_ref[pl.ds(n, PAIR)] = acc.reshape(PAIR, PAGE, HEAD)
+
+    def units(r, first, last):
+        for dc in range(2):
+            if first <= 2 * dc < last:
+
+                @pl.loop(1 - dc, NY)
+                def _(dy):
+                    deliver(r, 2 * dy + dc).wait_recv()
+
+            lo, hi = max(first, 2 * dc), min(last, 2 * dc + 2)
+            if lo < hi:
+
+                @pl.loop(lo - 2 * dc, hi - 2 * dc)
+                def _(h):
+                    attend(r, dc, h)
+
+    find()
+    new_tokens()
+    ring(0, 2)
+    ring(2, 1)
+    ring(0, 3)
+    ring(1, 2)
+    ring(3, 1)
+    ring(0, 4)
+    ring(1, 3)
+    ring(2, 2)
+    hand_out(0)
+    ring(1, 4)
+    ring(2, 3)
+    units(0, 0, 2)
+    hand_out(1)
+    ring(3, 2)
+    units(0, 2, 4)
+    ring(2, 4)
+    units(1, 0, 1)
+    ring(3, 3)
+    units(1, 1, 2)
+    hand_out(2)
+    ring(3, 4)
+    units(1, 2, 4)
+    hand_out(3)
+    units(2, 0, 4)
+    units(3, 0, 4)
+
+    for n in range(KV_HEADS * GROUP):
+        total = jnp.sum(l_ref[n], axis=1, keepdims=True)
+        out_ref[:, n * HEAD:(n + 1) * HEAD] = (acc_ref[n] / total).astype(jnp.bfloat16)
+
+    for r in range(ROUNDS):
+
+        @pl.loop(1, 2 * NY)
+        def _(k):
+            spread(r, k).wait_send()
+            deliver(r, k).wait_send()
+
+        for s in range(2):
+            for t in range(1, HOPS + 1):
+                hop(r, s, t).wait_send()
+
+
+def narrow(queries, new_keys, fresh_values, lent_page_pool, page_lender, page_slot, starts):
+    lender = page_lender[:, 0]
+    page = (lender // 2 % NZ) * PLANE + (lender // (2 * NZ) * 2 + lender % 2) * SLOTS + page_slot
+    table = jnp.broadcast_to(page[:, None] + 1, (8, 128))
+    vmem, smem, hbm = (pl.BlockSpec(memory_space=space) for space in (pltpu.VMEM, pltpu.SMEM, pl.ANY))
+    dma = pltpu.SemaphoreType.DMA
+    heads = KV_HEADS * GROUP
+    bf16, f32, i32 = jnp.bfloat16, jnp.float32, jnp.int32
+    tiles = lambda *n: pltpu.VMEM((*n, ROWS, HEAD), bf16)
+    ints = lambda *n: pltpu.VMEM((*n, 8, 128), i32)
+    return pl.pallas_call(
+        narrow_kernel,
+        out_shape=(jax.ShapeDtypeStruct(queries.shape, bf16), jax.ShapeDtypeStruct((1, 1), i32)),
+        in_specs=[smem, vmem, hbm, hbm, hbm, hbm],
+        out_specs=(vmem, smem),
+        scratch_shapes=[
+            pltpu.VMEM(queries.shape, bf16), pltpu.VMEM(new_keys.shape, bf16), pltpu.VMEM(fresh_values.shape, bf16),
+            tiles(NY, 2, ROUNDS, SLOTS),
+            [tiles(PLANE) for _ in range(ROUNDS)],
+            [[[tiles(width(r, t + 1)) for t in range(HOPS)] for _ in range(2)] for r in range(ROUNDS)],
+            tiles(ROUNDS, 2, TOTAL), tiles(JOINED),
+            tiles(ROUNDS, 2 * NY, CTX_PAGES), tiles(ROUNDS, 2 * NY, CTX_PAGES),
+            ints(NX), ints(NZ), ints(2 * NY), ints(2), pltpu.SMEM((2, 8, 128), i32),
+            ints(NZ), ints(2 * HOPS), ints(2 * HOPS), ints(2 * HOPS), pltpu.VMEM((128, 128), i32),
+            ints(4), pltpu.SMEM((4, 8, 128), i32), pltpu.SMEM((16, 128), i32),
+            pltpu.VMEM((heads, PAGE, HEAD), f32), pltpu.VMEM((heads, PAGE, HEAD), f32), pltpu.VMEM((heads, PAGE, HEAD), f32),
+            dma((3,)), dma, dma((ROUNDS,)), dma((2,)),
+            dma((NX,)), dma((NX,)), dma((NZ,)), dma((NZ,)), dma((2 * NY,)), dma((2 * NY,)),
+            dma((ROUNDS, 2 * NY)), dma((ROUNDS, 2 * NY)),
+            dma((ROUNDS, 2, HOPS)), dma((ROUNDS, 2, HOPS)),
+            dma((ROUNDS, 2 * NY)), dma((ROUNDS, 2 * NY)),
+        ],
+        compiler_params=pltpu.CompilerParams(
+            collective_id=1, has_side_effects=True, vmem_limit_bytes=56 * 1024 * 1024
+        ),
+        cost_estimate=pl.CostEstimate(
+            flops=4 * heads * PAGE * HEAD * (CTX_PAGES + 1) * PAGE,
+            bytes_accessed=4 << 20,
+            transcendentals=heads * PAGE * (CTX_PAGES + 1) * PAGE,
+        ),
+    )(starts, table, queries, new_keys, fresh_values, lent_page_pool)
+
+
+def wide(queries, new_keys, fresh_values, lent_page_pool, page_lender, page_slot, starts):
     pages = page_lender * SLOTS + page_slot[:, None]
     table = jnp.broadcast_to(pages, (8, 128))
     vmem = pl.BlockSpec(memory_space=pltpu.VMEM)
@@ -223,7 +660,7 @@
     heads = KV_HEADS * GROUP
     bf16, f32, i32 = jnp.bfloat16, jnp.float32, jnp.int32
     return pl.pallas_call(
-        kernel,
+        wide_kernel,
         out_shape=jax.ShapeDtypeStruct(queries.shape, bf16),
         in_specs=[
             pl.BlockSpec(memory_space=pltpu.SMEM), vmem, vmem, vmem, pl.BlockSpec(memory_space=pl.ANY), vmem,
@@ -259,6 +696,11 @@
     )(starts, queries, new_keys, fresh_values, lent_page_pool, table)
 
 
+def local(*args):
+    out, over = narrow(*args)
+    return lax.cond(over[0, 0] > 0, lambda: wide(*args), lambda: out)
+
+
 def solution(mesh):
     in_specs = (
         P("inst", "tp"),

time: 178 us -> 139 us (0.78)
  the two profiles are of different devices: /device:TPU:50 before, /device:TPU:1 now
where the time goes in v2:
time: 139 us; the launch traced here: 138 us
  Pallas kernels  134 us (96%)
  local copies, waits for them, and re-layouts  1.49 us (1%)
  between operations  1.42 us (1%)
    pallas_call x1, Pallas kernels, narrow(): pl.pallas_call(narrow_kernel, out_shape=(jax.ShapeDtypeStruct(queries.sha...  134 us

profile of v2, /device:TPU:1, one launch (start us, length us, event | category | flops | bytes accessed | tf_op | source)
XLA Modules:
  0.0 137.8 jit_solution(17659183221686374497)
XLA Ops:
  0.7 0.7 fusion.6
  1.3 0.7 broadcast_in_dim.16.tab_ref
  2.0 0.0 copy-start
  2.0 0.0 copy-start.1
  2.0 0.0 copy-start.2
  2.0 0.0 copy-start.3
  2.0 0.0 copy-start.4
  2.0 0.0 copy-start.5
  2.0 134.0 %shard_map.75 = (bf16[128,2048]{1,0:T(8,128)(2,1)S(1)}, s32[1,1]{1,0:T(1,128)}) custom-call(s32[1]{0:T(128)S(6)} %copy.13.start_ref, s32[8,128]{1,0:T(8,128)} %broadcast_in_dim.16.tab_ref, bf16[128,2048]{1,0:T(8,128)(2,1)} %q_any.1, bf16[128,256]{1,0:T(8,128)(2,1)} %nk_any.1, bf16[128,256]{1,0:T(8,128)(2,1)} %nv_any.1, bf16[16,2,128,256]{3,2,1,0:T(8,128)(2,1)} %pool_ref.1), custom_call_target="tpu_custom_call" | custom-call | flops 4429185024 | bytes 4194304 | tf_op jit(solution)/shard_map/pallas_call | solution.py:622
  136.8 0.0 copy-done
  136.8 0.0 copy-done.1
  136.8 0.0 copy-done.2
  136.8 0.0 copy-done.3
  136.8 0.0 copy-done.4
  136.8 0.0 copy-done.5
  136.8 0.2 conditional.1
  137.0 0.8 copy.14
Async XLA Ops:
  2.0 134.8 %copy-start = (bf16[16,2,128,256]{3,2,1,0:T(8,128)(2,1)S(1)}, bf16[16,2,128,256]{3,2,1,0:T(8,128)(2,1)}, u32[]{:S(2)}) copy-start(bf16[16,2,128,256]{3,2,1,0:T(8,128)(2,1)} %pool_ref.1) | copy-start | bytes 6291460
  2.0 134.8 %copy-start.1 = (bf16[128,2048]{1,0:T(8,128)(2,1)S(1)}, bf16[128,2048]{1,0:T(8,128)(2,1)}, u32[]{:S(2)}) copy-start(bf16[128,2048]{1,0:T(8,128)(2,1)} %q_any.1) | copy-start | bytes 1572868
  2.0 134.8 %copy-start.2 = (bf16[128,256]{1,0:T(8,128)(2,1)S(1)}, bf16[128,256]{1,0:T(8,128)(2,1)}, u32[]{:S(2)}) copy-start(bf16[128,256]{1,0:T(8,128)(2,1)} %nk_any.1) | copy-start | bytes 196612
  2.0 134.8 %copy-start.3 = (bf16[128,256]{1,0:T(8,128)(2,1)S(1)}, bf16[128,256]{1,0:T(8,128)(2,1)}, u32[]{:S(2)}) copy-start(bf16[128,256]{1,0:T(8,128)(2,1)} %nv_any.1) | copy-start | bytes 196612
  2.0 134.8 %copy-start.4 = (s32[8]{0:T(128)S(1)}, s32[8]{0:T(128)}, u32[]{:S(2)}) copy-start(s32[8]{0:T(128)} %param.14) | copy-start | bytes 100
  2.0 134.8 %copy-start.5 = (s32[8,1]{0,1:T(1,128)S(1)}, s32[8,1]{0,1:T(1,128)}, u32[]{:S(2)}) copy-start(s32[8,1]{0,1:T(1,128)} %param.13) | copy-start | bytes 100

commit v3 on v2

--- a/solution.py
+++ b/solution.py
@@ -218,10 +218,10 @@
 
 
 ROUNDS = 4
-OPEN = 2
+OPEN = 1
 PLANE = 2 * NY * SLOTS
-WIDTH = (84, 72, 56, 24)
-OFF = (0, 128, 200, 256)
+WIDTH = (84, 70, 54, 24)
+OFF = (0, 128, 198, 252)
 TOTAL = OFF[-1] + WIDTH[-1]
 JOINED = PLANE + 2 * TOTAL
 HOPS = len(WIDTH)
@@ -232,15 +232,19 @@
     return PLANE if t == 1 and r < OPEN else WIDTH[t - 1]
 
 
+def step_of(n, most):
+    return max(d for d in range(1, most + 1) if n % d == 0)
+
+
 def base_of(s, t):
     return PLANE + s * TOTAL + OFF[t - 1]
 
 
 def narrow_kernel(
-    start_ref, tab_ref, q_any, nk_any, nv_any, pool_ref, out_ref, over_ref,
+    start_ref, lender_ref, slot_ref, q_any, nk_any, nv_any, pool_ref, out_ref, over_ref,
     q_ref, nk_ref, nv_ref, stage, home, arrive, sbuf, join, ybuf, recv,
     tabx, tabz, tabp, tabv, tabs, need, member, before, place, mat, metav, meta, plist, m_ref, l_ref, acc_ref,
-    in_sem, load_sem, own_sem, smem_sem, xs, xr, zs, zr, ps, pr, hs, hr, rs, rr, ys, yr,
+    in_sem, load_sem, own_sem, smem_sem, ms, mr, xs, xr, zs, zr, ps, pr, hs, hr, rs, rr, ys, yr,
 ):
     inst, x = lax.axis_index("inst"), lax.axis_index("tp")
     core, chip = inst % 2, inst // 2
@@ -259,14 +263,18 @@
         pltpu.make_async_copy(src, dst, in_sem.at[n])
         for n, (src, dst) in enumerate(((q_any, q_ref), (nk_any, nk_ref), (nv_any, nv_ref)))
     ]
-    for yy in range(NY):
-        for tb in range(NZ):
-            pltpu.make_async_copy(
-                pool_ref.at[:, yy % 2, pl.ds(tb * ROWS, ROWS), pl.ds((yy // 2) * HEAD, HEAD)],
-                stage.at[yy, tb % 2, tb // 2], load_sem,
-            ).start()
-    for copy in inputs:
-        copy.start()
+    def load_all(r):
+        for yy in range(NY):
+            for half in range(2):
+                pltpu.make_async_copy(
+                    pool_ref.at[:, yy % 2, pl.ds((2 * r + half) * ROWS, ROWS), pl.ds((yy // 2) * HEAD, HEAD)],
+                    stage[r].at[yy, half], load_sem.at[r],
+                ).start()
+
+    def loaded(r):
+        pltpu.make_async_copy(stage[r], stage[r], load_sem.at[r]).wait()
+
+    load_all(0)
 
     barrier = pltpu.get_barrier_semaphore()
 
@@ -289,7 +297,12 @@
     row = lax.broadcasted_iota(i32, (8, 128), 0)
     lane = lax.broadcasted_iota(i32, (8, 128), 1)
     wanted = (lane == chip * NX + x) & ((x * 8 + row) * PAGE < start_ref[0])
-    tabx[0] = jnp.where(wanted, tab_ref[...], 0)
+    named = jnp.zeros((8, 128), i32)
+    for e in range(8):
+        lender = lender_ref[e, 0]
+        page = (lender // 2 % NZ) * PLANE + (lender // (2 * NZ) * 2 + lender % 2) * SLOTS + slot_ref[e]
+        named = jnp.where(row == e, page + 1, named)
+    tabx[0] = jnp.where(wanted, named, 0)
 
     def table_x(d):
         return remote(tabx.at[0], tabx.at[d], xs.at[d], xr.at[d], (inst, (x + d) % NX))
@@ -297,17 +310,16 @@
     for d in range(1, NX):
         table_x(d).start()
 
-    pltpu.make_async_copy(stage, stage, load_sem).wait()
     here = pl.ds((y * 2 + core) * SLOTS, SLOTS)
 
     def spread(r, k):
         dy, dc = k // 2, k % 2
         return remote(
-            stage.at[(y + dy) % NY, (core + dc) % 2, r], home[r].at[here], hs.at[r, k], hr.at[r, k], device(dy, 0, dc)
+            stage[r].at[(y + dy) % NY, (core + dc) % 2], home[r].at[here], hs.at[r, k], hr.at[r, k], device(dy, 0, dc)
         )
 
     def own(r):
-        return pltpu.make_async_copy(stage.at[y, core, r], home[r].at[here], own_sem.at[r])
+        return pltpu.make_async_copy(stage[r].at[y, core], home[r].at[here], own_sem.at[r])
 
     def spread_all(r):
         own(r).start()
@@ -319,6 +331,30 @@
     def hop(r, s, t):
         src = home[r] if width(r, t) == PLANE else sbuf.at[r, s, pl.ds(OFF[t - 1], WIDTH[t - 1])]
         return remote(src, arrive[r][s][t - 1], rs.at[r, s, t - 1], rr.at[r, s, t - 1], device(0, STEP[s], 0))
+
+    def piece(s, k):
+        part = pl.ds(((y - k // 2 + NY) % NY * 2 + (core + k % 2) % 2) * SLOTS, SLOTS)
+        return remote(
+            home[0].at[part], arrive[0][s][0].at[part], ms.at[s, k], mr.at[s, k], device(0, STEP[s], 0)
+        )
+
+    def send_piece(k):
+        if k == 0:
+            own(0).wait()
+        else:
+            spread(0, k).wait_recv()
+        for s in range(2):
+            piece(s, k).start()
+
+    def wait_hop(r, s, t):
+        if r == 0 and t == 1:
+
+            @pl.loop(0, 2 * NY)
+            def _(k):
+                piece(s, k).wait_recv()
+
+        else:
+            hop(r, s, t).wait_recv()
 
     def ring(r, t):
         if t == 1:
@@ -332,20 +368,23 @@
         for s in range(2):
             source = home[r]
             if t > 1:
-                hop(r, s, t - 1).wait_recv()
+                wait_hop(r, s, t - 1)
                 source = arrive[r][s][t - 2]
             if width(r, t) < PLANE:
 
-                @pl.loop(0, WIDTH[t - 1] // 4)
+                some = step_of(WIDTH[t - 1], 8)
+
+                @pl.loop(0, WIDTH[t - 1] // some)
                 def _(kk):
-                    for u in range(4):
-                        k = kk * 4 + u
+                    for u in range(some):
+                        k = kk * some + u
                         sbuf[r, s, OFF[t - 1] + k] = source[meta[lists, s * HOPS + t - 1, k]]
 
             hop(r, s, t).start()
 
+    loaded(0)
     spread_all(0)
-
+    send_piece(0)
     for d in range(1, NX):
         table_x(d).wait()
     tabz[0] = tabx[0] + tabx[1] + tabx[2] + tabx[3]
@@ -357,6 +396,14 @@
     def _(d):
         table_z(d).start()
 
+    send_piece(1)
+    for r in range(1, ROUNDS):
+        load_all(r)
+    for copy in inputs:
+        copy.start()
+    for k in (2, 6, 3, 7):
+        send_piece(k)
+
     @pl.loop(1, NZ)
     def _(d):
         table_z(d).wait()
@@ -370,8 +417,33 @@
     def _(k):
         table_p(k).start()
 
+    loaded(1)
     spread_all(1)
-    ring(0, 1)
+    for k in (4, 5):
+        send_piece(k)
+
+    def new_tokens():
+        for copy in inputs:
+            copy.wait()
+        rows_ = lax.broadcasted_iota(i32, (GROUP * PAGE, PAGE), 0) % PAGE
+        cols_ = lax.broadcasted_iota(i32, (GROUP * PAGE, PAGE), 1)
+
+        @pl.loop(0, KV_HEADS)
+        def _(h):
+            head = pl.ds(pl.multiple_of(h * HEAD, HEAD), HEAD)
+            n = pl.ds(h * GROUP, GROUP)
+            q = jnp.concatenate(
+                [q_ref[:, pl.ds(pl.multiple_of((h * GROUP + e) * HEAD, HEAD), HEAD)] for e in range(GROUP)], axis=0
+            )
+            s = jnp.where(cols_ <= rows_, scores(q, nk_ref[:, head]), -jnp.inf)
+            m = jnp.broadcast_to(jnp.max(s, axis=1, keepdims=True), s.shape)
+            p = jnp.exp2(s - m)
+            m_ref[n] = m.reshape(GROUP, PAGE, HEAD)
+            l_ref[n] = p.reshape(GROUP, PAGE, HEAD)
+            acc = jnp.dot(p.astype(jnp.bfloat16), nv_ref[:, head], preferred_element_type=jnp.float32)
+            acc_ref[n] = acc.reshape(GROUP, PAGE, HEAD)
+
+    new_tokens()
 
     @pl.loop(1, 2 * NY)
     def _(k):
@@ -381,9 +453,6 @@
         tabv[dc] = functools.reduce(jnp.add, [tabp[2 * dy + dc] for dy in range(NY)])
     to_smem = pltpu.make_async_copy(tabv, tabs, smem_sem.at[0])
     to_smem.start()
-    ring(1, 1)
-    for r in range(2, ROUNDS):
-        spread_all(r)
     to_smem.wait()
 
     number = row * PLANE + lane + 1
@@ -397,6 +466,9 @@
                     for e in range(8):
                         hit = jnp.where(number == tabs[dc, e, (yy * NZ + d) * NX + xx], 1, hit)
         need[d] = hit
+
+    if OPEN > 1:
+        ring(1, 1)
 
     def ahead(k):
         return functools.reduce(jnp.add, [jnp.where(row == (d - k) % NZ, need[d], 0) for d in range(NZ)])
@@ -468,19 +540,22 @@
         return remote(ybuf.at[r, k], recv.at[r, k], ys.at[r, k], yr.at[r, k], device(k // 2, 0, k % 2))
 
     def hand_out(r):
-        for s in range(2):
-            hop(r, s, HOPS).wait_recv()
+        def gather(s, t):
+            some = step_of(width(r, t), 16)
+
+            @pl.loop(0, width(r, t) // some)
+            def _(j):
+                join[pl.ds(base_of(s, t) + j * some, some)] = arrive[r][s][t - 1][pl.ds(j * some, some)]
 
         @pl.loop(0, PLANE // 8)
         def _(j):
             join[pl.ds(j * 8, 8)] = home[r][pl.ds(j * 8, 8)]
 
-        for s in range(2):
-            for t in range(1, HOPS + 1):
-
-                @pl.loop(0, width(r, t) // 4)
-                def _(j):
-                    join[pl.ds(base_of(s, t) + j * 4, 4)] = arrive[r][s][t - 1][pl.ds(j * 4, 4)]
+        for t in range(1, HOPS + 1):
+            for s in range(2):
+                if t == HOPS:
+                    hop(r, s, HOPS).wait_recv()
+                gather(s, t)
 
         lists = 2 * NY if r < OPEN else 0
 
@@ -499,25 +574,6 @@
 
         for p in range(CTX_PAGES):
             recv[r, 0, p] = join[plist[lists, p]]
-
-    def new_tokens():
-        for copy in inputs:
-            copy.wait()
-        rows_ = lax.broadcasted_iota(i32, (PAGE, PAGE), 0)
-        cols_ = lax.broadcasted_iota(i32, (PAGE, PAGE), 1)
-        for h in range(KV_HEADS):
-            heads = pl.ds(h * HEAD, HEAD)
-
-            @pl.loop(0, GROUP, unroll=UNROLL)
-            def _(g):
-                n = h * GROUP + g
-                q = q_ref[:, pl.ds(pl.multiple_of(n * HEAD, HEAD), HEAD)]
-                s = jnp.where(cols_ <= rows_, scores(q, nk_ref[:, heads]), -jnp.inf)
-                m = jnp.broadcast_to(jnp.max(s, axis=1, keepdims=True), s.shape)
-                p = jnp.exp2(s - m)
-                m_ref[n] = m
-                l_ref[n] = p
-                acc_ref[n] = jnp.dot(p.astype(jnp.bfloat16), nv_ref[:, heads], preferred_element_type=jnp.float32)
 
     start = start_ref[0]
     keys = CTX_PAGES * ROWS
@@ -565,10 +621,14 @@
                 def _(h):
                     attend(r, dc, h)
 
-    find()
-    new_tokens()
+    if OPEN == 1:
+        ring(1, 1)
+    for r in range(2, ROUNDS):
+        loaded(r)
+        spread_all(r)
     ring(0, 2)
     ring(2, 1)
+    find()
     ring(0, 3)
     ring(1, 2)
     ring(3, 1)
@@ -595,7 +655,7 @@
 
     for n in range(KV_HEADS * GROUP):
         total = jnp.sum(l_ref[n], axis=1, keepdims=True)
-        out_ref[:, n * HEAD:(n + 1) * HEAD] = (acc_ref[n] / total).astype(jnp.bfloat16)
+        out_ref[:, n * HEAD:(n + 1) * HEAD] = (acc_ref[n] * (1.0 / total)).astype(jnp.bfloat16)
 
     for r in range(ROUNDS):
 
@@ -606,13 +666,17 @@
 
         for s in range(2):
             for t in range(1, HOPS + 1):
-                hop(r, s, t).wait_send()
+                if r == 0 and t == 1:
+
+                    @pl.loop(0, 2 * NY)
+                    def _(k):
+                        piece(s, k).wait_send()
+
+                else:
+                    hop(r, s, t).wait_send()
 
 
 def narrow(queries, new_keys, fresh_values, lent_page_pool, page_lender, page_slot, starts):
-    lender = page_lender[:, 0]
-    page = (lender // 2 % NZ) * PLANE + (lender // (2 * NZ) * 2 + lender % 2) * SLOTS + page_slot
-    table = jnp.broadcast_to(page[:, None] + 1, (8, 128))
     vmem, smem, hbm = (pl.BlockSpec(memory_space=space) for space in (pltpu.VMEM, pltpu.SMEM, pl.ANY))
     dma = pltpu.SemaphoreType.DMA
     heads = KV_HEADS * GROUP
@@ -622,11 +686,11 @@
     return pl.pallas_call(
         narrow_kernel,
         out_shape=(jax.ShapeDtypeStruct(queries.shape, bf16), jax.ShapeDtypeStruct((1, 1), i32)),
-        in_specs=[smem, vmem, hbm, hbm, hbm, hbm],
+        in_specs=[smem, smem, smem, hbm, hbm, hbm, hbm],
         out_specs=(vmem, smem),
         scratch_shapes=[
             pltpu.VMEM(queries.shape, bf16), pltpu.VMEM(new_keys.shape, bf16), pltpu.VMEM(fresh_values.shape, bf16),
-            tiles(NY, 2, ROUNDS, SLOTS),
+            [tiles(NY, 2, SLOTS) for _ in range(ROUNDS)],
             [tiles(PLANE) for _ in range(ROUNDS)],
             [[[tiles(width(r, t + 1)) for t in range(HOPS)] for _ in range(2)] for r in range(ROUNDS)],
             tiles(ROUNDS, 2, TOTAL), tiles(JOINED),
@@ -635,7 +699,7 @@
             ints(NZ), ints(2 * HOPS), ints(2 * HOPS), ints(2 * HOPS), pltpu.VMEM((128, 128), i32),
             ints(4), pltpu.SMEM((4, 8, 128), i32), pltpu.SMEM((16, 128), i32),
             pltpu.VMEM((heads, PAGE, HEAD), f32), pltpu.VMEM((heads, PAGE, HEAD), f32), pltpu.VMEM((heads, PAGE, HEAD), f32),
-            dma((3,)), dma, dma((ROUNDS,)), dma((2,)),
+            dma((3,)), dma((ROUNDS,)), dma((ROUNDS,)), dma((2,)), dma((2, 2 * NY)), dma((2, 2 * NY)),
             dma((NX,)), dma((NX,)), dma((NZ,)), dma((NZ,)), dma((2 * NY,)), dma((2 * NY,)),
             dma((ROUNDS, 2 * NY)), dma((ROUNDS, 2 * NY)),
             dma((ROUNDS, 2, HOPS)), dma((ROUNDS, 2, HOPS)),
@@ -649,7 +713,7 @@
             bytes_accessed=4 << 20,
             transcendentals=heads * PAGE * (CTX_PAGES + 1) * PAGE,
         ),
-    )(starts, table, queries, new_keys, fresh_values, lent_page_pool)
+    )(starts, page_lender, page_slot, queries, new_keys, fresh_values, lent_page_pool)
 
 
 def wide(queries, new_keys, fresh_values, lent_page_pool, page_lender, page_slot, starts):

time: 139 us -> 133 us (0.957)
  Pallas kernels: 134 us -> 129 us
    pallas_call x1, Pallas kernels: 134 us -> 129 us  [narrow(): pl.pallas_call(narrow_kernel, out_shape=(jax.ShapeDtypeStruct(queries.sha...]
where the time goes in v3:
time: 133 us; the launch traced here: 132 us
  Pallas kernels  129 us (97%)
  local copies, waits for them, and re-layouts  2.15 us (2%)
  between operations  1.42 us (1%)
    pallas_call x1, Pallas kernels, narrow(): pl.pallas_call(narrow_kernel, out_shape=(jax.ShapeDtypeStruct(queries.sha...  129 us

profile of v3, /device:TPU:1, one launch (start us, length us, event | category | flops | bytes accessed | tf_op | source)
XLA Modules:
  0.0 132.4 jit_solution(4343354537546253604)
XLA Ops:
  0.7 1.3 copy.10.lender_ref
  2.0 0.0 copy-start
  2.0 0.0 copy-start.1
  2.0 0.0 copy-start.2
  2.0 0.0 copy-start.3
  2.0 0.0 copy-start.4
  2.0 0.0 copy-start.5
  2.0 128.8 %shard_map.75 = (bf16[128,2048]{1,0:T(8,128)(2,1)S(1)}, s32[1,1]{1,0:T(1,128)}) custom-call(s32[1]{0:T(128)S(6)} %copy.14.start_ref, s32[8,1]{1,0:T(8,128)} %copy.10.lender_ref, s32[8]{0:T(128)} %slot_ref.1, bf16[128,2048]{1,0:T(8,128)(2,1)} %q_any.1, bf16[128,256]{1,0:T(8,128)(2,1)} %nk_any.1, bf16[128,256]{1,0:T(8,128)(2,1)} %nv_any.1, ...), custom_call_target="tpu_custom_call" | custom-call | flops 4429185024 | bytes 4194304 | tf_op jit(solution)/shard_map/pallas_call | solution.py:686
  131.5 0.0 copy-done
  131.5 0.0 copy-done.1
  131.5 0.0 copy-done.2
  131.6 0.0 copy-done.3
  131.6 0.0 copy-done.4
  131.6 0.0 copy-done.5
  131.6 0.8 copy.15
  (1 shorter events, 0.0 us)
Async XLA Ops:
  2.0 129.6 %copy-start = (s32[8,1]{0,1:T(1,128)S(1)}, s32[8,1]{0,1:T(1,128)}, u32[]{:S(2)}) copy-start(s32[8,1]{0,1:T(1,128)} %param.13) | copy-start | bytes 100
  2.0 129.6 %copy-start.1 = (bf16[16,2,128,256]{3,2,1,0:T(8,128)(2,1)S(1)}, bf16[16,2,128,256]{3,2,1,0:T(8,128)(2,1)}, u32[]{:S(2)}) copy-start(bf16[16,2,128,256]{3,2,1,0:T(8,128)(2,1)} %pool_ref.1) | copy-start | bytes 6291460
  2.0 129.6 %copy-start.2 = (bf16[128,2048]{1,0:T(8,128)(2,1)S(1)}, bf16[128,2048]{1,0:T(8,128)(2,1)}, u32[]{:S(2)}) copy-start(bf16[128,2048]{1,0:T(8,128)(2,1)} %q_any.1) | copy-start | bytes 1572868
  2.0 129.6 %copy-start.3 = (bf16[128,256]{1,0:T(8,128)(2,1)S(1)}, bf16[128,256]{1,0:T(8,128)(2,1)}, u32[]{:S(2)}) copy-start(bf16[128,256]{1,0:T(8,128)(2,1)} %nk_any.1) | copy-start | bytes 196612
  2.0 129.6 %copy-start.4 = (bf16[128,256]{1,0:T(8,128)(2,1)S(1)}, bf16[128,256]{1,0:T(8,128)(2,1)}, u32[]{:S(2)}) copy-start(bf16[128,256]{1,0:T(8,128)(2,1)} %nv_any.1) | copy-start | bytes 196612
  2.0 129.6 %copy-start.5 = (s32[8]{0:T(128)S(1)}, s32[8]{0:T(128)}, u32[]{:S(2)}) copy-start(s32[8]{0:T(128)} %slot_ref.1) | copy-start | bytes 100

commit v4 on v3

--- a/solution.py
+++ b/solution.py
@@ -274,8 +274,6 @@
     def loaded(r):
         pltpu.make_async_copy(stage[r], stage[r], load_sem.at[r]).wait()
 
-    load_all(0)
-
     barrier = pltpu.get_barrier_semaphore()
 
     def greet(dev):
@@ -292,7 +290,7 @@
     def _(k):
         greet(device(k // 2, 0, k % 2))
 
-    pl.semaphore_wait(barrier, NX - 1 + NZ - 1 + 2 * NY - 1)
+    load_all(0)
 
     row = lax.broadcasted_iota(i32, (8, 128), 0)
     lane = lax.broadcasted_iota(i32, (8, 128), 1)
@@ -303,6 +301,8 @@
         page = (lender // 2 % NZ) * PLANE + (lender // (2 * NZ) * 2 + lender % 2) * SLOTS + slot_ref[e]
         named = jnp.where(row == e, page + 1, named)
     tabx[0] = jnp.where(wanted, named, 0)
+
+    pl.semaphore_wait(barrier, NX - 1 + NZ - 1 + 2 * NY - 1)
 
     def table_x(d):
         return remote(tabx.at[0], tabx.at[d], xs.at[d], xr.at[d], (inst, (x + d) % NX))
@@ -539,6 +539,9 @@
     def deliver(r, k):
         return remote(ybuf.at[r, k], recv.at[r, k], ys.at[r, k], yr.at[r, k], device(k // 2, 0, k % 2))
 
+    def near_first(j):
+        return 1 + 2 * j - 3 * (j // 2)
+
     def hand_out(r):
         def gather(s, t):
             some = step_of(width(r, t), 16)
@@ -564,13 +567,15 @@
                 ybuf[r, k, p] = join[plist[lists + k, p]]
             deliver(r, k).start()
 
-        @pl.loop(1, NY)
-        def _(dy):
-            pick(2 * dy)
-
-        @pl.loop(0, NY)
-        def _(dy):
-            pick(2 * dy + 1)
+        @pl.loop(0, NY - 1)
+        def _(j):
+            pick(2 * near_first(j))
+
+        pick(1)
+
+        @pl.loop(0, NY - 1)
+        def _(j):
+            pick(2 * near_first(j) + 1)
 
         for p in range(CTX_PAGES):
             recv[r, 0, p] = join[plist[lists, p]]
@@ -651,29 +656,42 @@
     units(1, 2, 4)
     hand_out(3)
     units(2, 0, 4)
-    units(3, 0, 4)
+    for r in range(ROUNDS):
+
+        @pl.loop(1, 2 * NY)
+        def _(k):
+            spread(r, k).wait_send()
+            if r < ROUNDS - 1:
+                deliver(r, k).wait_send()
+
+        for s in range(2):
+            for t in range(1, HOPS + 1):
+                if r == 0 and t == 1:
+
+                    @pl.loop(0, 2 * NY)
+                    def _(k):
+                        piece(s, k).wait_send()
+
+                else:
+                    hop(r, s, t).wait_send()
+
+    pair_dy = (y % 2) + 3 * (1 - y % 2)
+    for dc in range(2):
+        if dc:
+            deliver(3, 1).wait_recv()
+        deliver(3, 2 * pair_dy + dc).wait_recv()
+        attend(3, dc, y // 2)
+        deliver(3, 2 * (4 - pair_dy) + dc).wait_recv()
+        deliver(3, 4 + dc).wait_recv()
+        attend(3, dc, 1 - y // 2)
 
     for n in range(KV_HEADS * GROUP):
         total = jnp.sum(l_ref[n], axis=1, keepdims=True)
         out_ref[:, n * HEAD:(n + 1) * HEAD] = (acc_ref[n] * (1.0 / total)).astype(jnp.bfloat16)
 
-    for r in range(ROUNDS):
-
-        @pl.loop(1, 2 * NY)
-        def _(k):
-            spread(r, k).wait_send()
-            deliver(r, k).wait_send()
-
-        for s in range(2):
-            for t in range(1, HOPS + 1):
-                if r == 0 and t == 1:
-
-                    @pl.loop(0, 2 * NY)
-                    def _(k):
-                        piece(s, k).wait_send()
-
-                else:
-                    hop(r, s, t).wait_send()
+    @pl.loop(1, 2 * NY)
+    def _(k):
+        deliver(ROUNDS - 1, k).wait_send()
 
 
 def narrow(queries, new_keys, fresh_values, lent_page_pool, page_lender, page_slot, starts):

time: 133 us -> 130 us (0.977)
  Pallas kernels: 129 us -> 127 us
    pallas_call x1, Pallas kernels: 129 us -> 127 us  [narrow(): pl.pallas_call(narrow_kernel, out_shape=(jax.ShapeDtypeStruct(queries.sha...]
where the time goes in v4:
time: 130 us
  Pallas kernels  127 us (98%)
  local copies, waits for them, and re-layouts  2.15 us (2%)
  between operations  1.42 us (1%)
    pallas_call x1, Pallas kernels, narrow(): pl.pallas_call(narrow_kernel, out_shape=(jax.ShapeDtypeStruct(queries.sha...  127 us

profile of v4, /device:TPU:1, one launch (start us, length us, event | category | flops | bytes accessed | tf_op | source)
XLA Modules:
  0.0 130.3 jit_solution(8797768041581268902)
XLA Ops:
  0.7 1.3 %copy.10.lender_ref = s32[8,1]{1,0:T(8,128)} copy(s32[8,1]{0,1:T(1,128)} %param.13) | data formatting | bytes 64 | tf_op args[4]
  2.0 0.0 copy-start
  2.0 0.0 copy-start.1
  2.0 0.0 copy-start.2
  2.0 0.0 copy-start.3
  2.0 0.0 copy-start.4
  2.0 0.0 copy-start.5
  2.0 126.7 %shard_map.75 = (bf16[128,2048]{1,0:T(8,128)(2,1)S(1)}, s32[1,1]{1,0:T(1,128)}) custom-call(s32[1]{0:T(128)S(6)} %copy.14.start_ref, s32[8,1]{1,0:T(8,128)} %copy.10.lender_ref, s32[8]{0:T(128)} %slot_ref.1, bf16[128,2048]{1,0:T(8,128)(2,1)} %q_any.1, bf16[128,256]{1,0:T(8,128)(2,1)} %nk_any.1, bf16[128,256]{1,0:T(8,128)(2,1)} %nv_any.1, ...), custom_call_target="tpu_custom_call" | custom-call | flops 4429185024 | bytes 4194304 | tf_op jit(solution)/shard_map/pallas_call | solution.py:704
  129.4 0.0 copy-done
  129.4 0.0 copy-done.1
  129.4 0.0 copy-done.2
  129.4 0.0 copy-done.3
  129.5 0.0 copy-done.4
  129.5 0.0 copy-done.5
  129.5 0.8 copy.15
  (1 shorter events, 0.0 us)
Async XLA Ops:
  2.0 127.4 %copy-start = (s32[8,1]{0,1:T(1,128)S(1)}, s32[8,1]{0,1:T(1,128)}, u32[]{:S(2)}) copy-start(s32[8,1]{0,1:T(1,128)} %param.13) | copy-start | bytes 100
  2.0 127.4 %copy-start.1 = (bf16[16,2,128,256]{3,2,1,0:T(8,128)(2,1)S(1)}, bf16[16,2,128,256]{3,2,1,0:T(8,128)(2,1)}, u32[]{:S(2)}) copy-start(bf16[16,2,128,256]{3,2,1,0:T(8,128)(2,1)} %pool_ref.1) | copy-start | bytes 6291460
  2.0 127.5 %copy-start.2 = (bf16[128,2048]{1,0:T(8,128)(2,1)S(1)}, bf16[128,2048]{1,0:T(8,128)(2,1)}, u32[]{:S(2)}) copy-start(bf16[128,2048]{1,0:T(8,128)(2,1)} %q_any.1) | copy-start | bytes 1572868
  2.0 127.5 %copy-start.3 = (bf16[128,256]{1,0:T(8,128)(2,1)S(1)}, bf16[128,256]{1,0:T(8,128)(2,1)}, u32[]{:S(2)}) copy-start(bf16[128,256]{1,0:T(8,128)(2,1)} %nk_any.1) | copy-start | bytes 196612
  2.0 127.5 %copy-start.4 = (bf16[128,256]{1,0:T(8,128)(2,1)S(1)}, bf16[128,256]{1,0:T(8,128)(2,1)}, u32[]{:S(2)}) copy-start(bf16[128,256]{1,0:T(8,128)(2,1)} %nv_any.1) | copy-start | bytes 196612
  2.0 127.5 %copy-start.5 = (s32[8]{0:T(128)S(1)}, s32[8]{0:T(128)}, u32[]{:S(2)}) copy-start(s32[8]{0:T(128)} %slot_ref.1) | copy-start | bytes 100
